TPU v7x, 32 devices: a whole 2x2x4 slice. The times are simulated.
32 devices in a mesh: parts: 2 (over y), view: 4 (over z), pix: 4 (over x, core).
Axes of the slice: x: 2, y: 2, z: 4, core: 2. Of those that a mesh axis runs over, the one named last changes fastest.
Arguments:
- descriptors: bfloat16 [8, 768, 256], P(('parts', 'view'), 'pix'), parts along dimension 0, may hold values from -6 to 6
- matches: int32 [8, 4, 768], P(('parts', 'view'), None, 'pix'), parts along dimension 0, may hold values from 0 to 767
Outputs:
- descriptor_grad: bfloat16 [8, 768, 256], P(('parts', 'view'), 'pix'), parts along dimension 0
- pixel_loss: float32 [8, 768], P(('parts', 'view'), 'pix'), parts along dimension 0
There are 2 independent parts, one for each index of `parts`. A program takes and returns all parts, laid end to end along the dimension named above; each array names one. Nothing has to cross between parts.
Inputs may be any that keep to these rules, and one draw needn't show every extreme that they name: `matches`: entries with a == b are not used.
All inputs are finite; a program needn't handle non-finite values.
Results may differ from a plain program's by a relative error of at most 0.0053.
Values may be sent and summed in bfloat16 or wider, within the bound.
A program may use at most 128 MiB of HBM per device.

v0:
```python
import math

import jax
import jax.numpy as jnp
from jax import lax
from jax.sharding import PartitionSpec as P

INV_TEMP = 1.0 / 0.07


def body(descriptors, matches):
    views = lax.axis_size("view")
    shard_rows = descriptors.shape[1]
    me_view = lax.axis_index("view")
    me_slot = lax.axis_index("pix")
    raw = descriptors[0].astype(jnp.float32)
    scale = lax.rsqrt(jnp.mean(raw * raw, axis=-1, keepdims=True) + 1e-06) / math.sqrt(
        raw.shape[-1]
    )
    unit = raw * scale
    normed = unit.astype(jnp.bfloat16)
    whole = lax.all_gather(normed, "pix", axis=0, tiled=True)
    links = lax.all_gather(matches[0], "pix", axis=1, tiled=True)
    shards = lax.all_gather(normed[None], "view", axis=0, tiled=True)
    column_ids = me_slot * shard_rows + jnp.arange(shard_rows, dtype=jnp.int32)
    view_ids = jnp.arange(views, dtype=jnp.int32)

    def hits(second):
        return links[second][:, None] == column_ids[None, :]

    def partial_stats(second):
        sim = INV_TEMP * lax.dot_general(
            whole, shards[second], (((1,), (1,)), ((), ())), preferred_element_type=jnp.float32
        )
        expo = jnp.exp(sim)
        return (expo, jnp.sum(expo, axis=1), jnp.sum(jnp.where(hits(second), sim, 0.0), axis=1))

    exps, part_totals, part_pos = lax.map(partial_stats, view_ids)
    totals, positives = lax.psum((part_totals, part_pos), "pix")
    own_totals = lax.dynamic_slice_in_dim(totals, me_slot * shard_rows, shard_rows, 1)
    own_pos = lax.dynamic_slice_in_dim(positives, me_slot * shard_rows, shard_rows, 1)
    valid = (view_ids != me_view)[:, None]
    pixel_loss = jnp.sum(jnp.where(valid, jnp.log(own_totals) - own_pos, 0.0), axis=0) / (views - 1)

    def weights(second, expo):
        wgt = expo / totals[second][:, None] - hits(second).astype(jnp.float32)
        return jnp.where(second != me_view, wgt, 0.0).astype(jnp.bfloat16)

    def column_of(wgt):
        return lax.dot_general(
            wgt, whole, (((0,), (0,)), ((), ())), preferred_element_type=jnp.float32
        )

    def both_terms(row_acc, items):
        second, expo = items
        wgt = weights(second, expo)
        row_acc = row_acc + jnp.dot(wgt, shards[second], preferred_element_type=jnp.float32)
        return (row_acc, column_of(wgt))

    row_acc, column_parts = lax.scan(
        both_terms, jnp.zeros(whole.shape, jnp.float32), (view_ids, exps)
    )
    column_term = lax.psum_scatter(column_parts, "view", scatter_dimension=0, tiled=True)[0]
    row_term = lax.psum_scatter(row_acc, "pix", scatter_dimension=0, tiled=True)
    unit_grad = INV_TEMP / (views - 1) * (row_term + column_term)
    along = jnp.sum(unit * unit_grad, axis=-1, keepdims=True)
    descriptor_grad = (scale * (unit_grad - unit * along)).astype(jnp.bfloat16)
    return (descriptor_grad[None], pixel_loss[None])


def solution(mesh):
    in_specs = (P(("parts", "view"), "pix", None), P(("parts", "view"), None, "pix"))
    out_specs = (P(("parts", "view"), "pix", None), P(("parts", "view"), "pix"))
    return jax.shard_map(body, mesh=mesh, in_specs=in_specs, out_specs=out_specs, check_vma=False)
```

profile of v0, /device:TPU:1, one launch (start us, length us, event | category | flops | bytes accessed | tf_op | source)
XLA Modules:
  0.0 151.3 jit_solution(8712491264483014530)
XLA Ops:
  7.2 0.0 reduce-scatter.3.cloned.1.call-start
  7.2 1.0 fusion.37
  8.2 1.0 fusion.32
  9.2 1.0 fusion.38
  10.3 7.8 %all_gather.10 = bf16[768,256]{1,0:T(8,128)(2,1)S(1)} all-gather(bf16[192,256]{1,0:T(8,128)(2,1)S(1)} %fusion.32), channel_id=1, replica_groups=mesh['parts'=2,'view'=4,'pix'=4] {'pix'}, dimensions={0}, use_global_device_ids=true | all-gather | bytes 491520 | tf_op jit(solution)/shard_map/all_gather | solution.py:22
  18.1 13.2 %all_gather.9 = bf16[4,192,256]{2,1,0:T(8,128)(2,1)S(1)} all-gather(bf16[1,192,256]{2,1,0:T(8,128)(2,1)S(1)} %fusion.38), channel_id=1, replica_groups=mesh['parts'=2,'view'=4,'pix'=4] {'view'}, dimensions={0}, use_global_device_ids=true | all-gather | bytes 491520 | tf_op jit(solution)/shard_map/all_gather | solution.py:24
  31.3 0.8 copy.5
  32.1 7.9 %all-gather = s32[1,4,768]{1,0,2:T(1,128)S(1)} all-gather(s32[1,4,192]{1,0,2:T(1,128)S(1)} %copy.5), channel_id=2, replica_groups=mesh['parts'=2,'view'=4,'pix'=4] {'pix'}, dimensions={2}, use_global_device_ids=true | all-gather | bytes 15360 | tf_op jit(solution)/shard_map/all_gather | solution.py:23
  39.9 0.1 copy.6
  40.1 15.9 %while.28 = (s32[]{:T(128)}, f32[4,768,192]{1,2,0:T(8,128)}, f32[4,768]{1,0:T(4,128)S(1)}, f32[4,768]{1,0:T(4,128)S(1)}, s32[4]{0:T(128)S(1)}, /*index=5*/bf16[4...) while((s32[]{:T(128)}, f32[4,768,192]{1,2,0:T(8,128)}, ...), condition=%wide.region_4.5_spmd.clone, body=%wide.region_1.4_spmd.clone.sunk | while | flops 76233408 | bytes 2303159 | solution.py:38
  40.1 0.6 dynamic_slice.74
  42.6 1.1 bitcast_dynamic-update-slice_fusion.2
  43.7 0.2 select_reduce_fusion.3
  43.9 0.1 dynamic_update_slice.27
  44.0 0.1 dynamic_update_slice.26
  44.0 0.6 dynamic_slice.74
  46.5 1.1 bitcast_dynamic-update-slice_fusion.2
  47.7 0.2 select_reduce_fusion.3
  47.8 0.1 dynamic_update_slice.27
  47.9 0.1 dynamic_update_slice.26
  48.0 0.6 dynamic_slice.74
  50.5 1.2 bitcast_dynamic-update-slice_fusion.2
  51.7 0.2 select_reduce_fusion.3
  51.8 0.1 dynamic_update_slice.27
  51.9 0.1 dynamic_update_slice.26
  52.0 0.6 dynamic_slice.74
  54.4 1.1 bitcast_dynamic-update-slice_fusion.2
  55.6 0.2 select_reduce_fusion.3
  55.8 0.1 dynamic_update_slice.27
  55.9 0.1 dynamic_update_slice.26
  56.0 10.1 %all-reduce = (f32[4,768]{1,0:T(4,128)S(1)}, f32[4,768]{1,0:T(4,128)S(1)}) all-reduce(f32[4,768]{1,0:T(4,128)S(1)} %get-tuple-element.110, f32[4,768]{1,0:T(4,128)S(1)} %get-tuple-element.113), channel_id=1, replica_groups=mesh['parts'=2,'view'=4,'pix'=4] {'pix'}, use_global_device_ids=true, to_apply=%region_5.6 | all-reduce | flops 6144 | bytes 49152 | tf_op jit(solution)/shard_map/psum | solution.py:39
  66.1 24.9 %while.29 = (s32[]{:T(128)}, f32[768,256]{1,0:T(8,128)S(1)}, f32[4,192,256]{2,1,0:T(8,128)}, s32[4]{0:T(128)S(1)}, s32[]{:T(128)}, /*index=5*/f32[4,768,192]{1,2...) while((s32[]{:T(128)}, f32[768,256]{1,0:T(8,128)S(1)}, ...), condition=%wide.region_7.8_spmd.clone, body=%wide.region_6.7_spmd.clone.sunk | while | flops 153157824 | bytes 6026460 | solution.py:60
  66.1 0.6 dynamic_slice.79
  69.2 1.1 constant_dynamic-slice_fusion.2
  70.3 0.3 copy.11
  70.6 1.2 fusion.54
  71.8 0.4 convolution_add_fusion.2
  72.3 0.6 dynamic_slice.79
  75.4 1.1 constant_dynamic-slice_fusion.2
  76.5 0.3 copy.11
  76.8 1.2 fusion.54
  78.1 0.4 convolution_add_fusion.2
  78.5 0.6 dynamic_slice.79
  81.7 1.1 constant_dynamic-slice_fusion.2
  82.8 0.3 copy.11
  83.0 1.2 fusion.54
  84.3 0.4 convolution_add_fusion.2
  84.7 0.6 dynamic_slice.79
  87.9 1.1 constant_dynamic-slice_fusion.2
  89.0 0.3 copy.11
  89.3 1.3 fusion.54
  90.5 0.4 convolution_add_fusion.2
  91.0 0.0 copy-start.1
  91.0 0.9 copy-done.1
  91.8 0.0 reduce-scatter.3.cloned.1.call-update
  91.9 0.0 reduce-scatter.5.cloned.1.call-start
  91.9 0.7 reduce-scatter.5.cloned.1.call-update
  92.6 0.1 select_reduce_fusion.1
  92.7 0.6 broadcast_multiply_fusion
  93.3 23.7 %reduce-scatter.3.cloned.1.call-done = f32[192,256]{1,0:T(8,128)} async-done(((f32[768,256]{1,0:T(8,128)}), f32[192,256]{1,0:T(8,128)}) %reduce-scatter.3.cloned.1.call-update) | async-done | bytes 196624 | tf_op jit(solution)/shard_map/reduce_scatter | solution.py:64
  117.0 24.4 %reduce-scatter.5.cloned.1.call-done = f32[1,192,256]{2,1,0:T(8,128)} async-done(((f32[4,192,256]{2,1,0:T(8,128)}), f32[1,192,256]{2,1,0:T(8,128)}) %reduce-scatter.5.cloned.1.call-update) | async-done | bytes 196624 | tf_op jit(solution)/shard_map/reduce_scatter | solution.py:63
  141.4 0.0 copy-done
  141.5 1.2 fusion.33
  142.7 1.8 %fusion.40 = bf16[1,192,256]{2,1,0:T(8,128)(2,1)} fusion(bf16[1,192,256]{2,1,0:T(8,128)(2,1)S(1)} %copy-done, f32[192]{0:T(256)S(1)} %fusion.33, f32[192]{0:T(256)S(1)} %rsqrt_multiply_fusion, f32[192,256]{1,0:T(8,128)} %reduce-scatter.3.cloned.1.call-done, f32[1,192,256]{2,1,0:T(8,128)} %reduce-scatter.5.cloned.1.call-done), kind=kLoop, calls=%fused_computation.54 | loop fusion | flops 393216 | bytes 591360 | tf_op jit(solution)/shard_map/broadcast_in_dim | solution.py:68
  (38 shorter events, 0.3 us)
Async XLA Ops:
  7.2 109.8 %reduce-scatter.3.cloned.1.call-start = ((), (), s32[]{:S(2)}) async-start(), calls=%async_computation.2 | async-start | bytes 983040 | tf_op jit(solution)/shard_map/reduce_scatter | solution.py:64
  66.1 75.4 %copy-start = (bf16[1,192,256]{2,1,0:T(8,128)(2,1)S(1)}, bf16[1,192,256]{2,1,0:T(8,128)(2,1)}, u32[]{:S(2)}) copy-start(bf16[1,192,256]{2,1,0:T(8,128)(2,1)} %param.6) | copy-start | bytes 294916
  91.0 0.9 copy-start.1
  91.9 49.6 %reduce-scatter.5.cloned.1.call-start = ((), (), s32[]{:S(2)}) async-start(), calls=%async_computation.3 | async-start | bytes 983040 | tf_op jit(solution)/shard_map/reduce_scatter | solution.py:63
Sparse Core Ops, SparseCore 0:
  92.0 24.9 reduce-scatter.2
  119.4 21.9 reduce-scatter.4
where the time goes:
time: 154 us; the launch traced here: 151 us
  waiting for transfers between devices  48.9 us (32%)
  blocking collectives  39 us (25%)
  loops' own time  17.9 us (12%)
  between operations  14.2 us (9%)
  local copies, waits for them, and re-layouts  12.8 us (8%)
  matrix products  11.2 us (7%)
  other arithmetic  7.3 us (5%)
    reduce_scatter x1, waiting for transfers between devices, body(): lax.psum_scatter(column_parts, 'view', scatter_dimension=0, tiled=True)[0]  24.4 us
    reduce_scatter x1, waiting for transfers between devices, body(): row_term = lax.psum_scatter(row_acc, 'pix', scatter_dimension=0, tiled=True)  23.7 us
    all_gather x1, blocking collectives, body(): shards = lax.all_gather(normed[None], 'view', axis=0, tiled=True)  13.2 us
    another operation x1, loops' own time, body(): lax.scan(both_terms, jnp.zeros(whole.shape, jnp.float32), (view_ids, exps))  10.2 us
    psum x1, blocking collectives, body(): totals, positives = lax.psum((part_totals, part_pos), 'pix')  10.1 us
    all_gather x1, blocking collectives, body(): links = lax.all_gather(matches[0], 'pix', axis=1, tiled=True)  7.88 us
    all_gather x1, blocking collectives, body(): whole = lax.all_gather(normed, 'pix', axis=0, tiled=True)  7.8 us
    another operation x1, loops' own time, body(): exps, part_totals, part_pos = lax.map(partial_stats, view_ids)  7.7 us
  transfers between devices with their start and end apart: 2, of which 2 were waited for; matrix products, arithmetic and copies ran while one was open for 0% of the time, Pallas kernels for 0%

commit v1 on v0

v1 whole, which is shorter than its diff:
```python
import functools
import math

import jax
import jax.numpy as jnp
from jax import lax
from jax.experimental import pallas as pl
from jax.experimental.pallas import tpu as pltpu
from jax.sharding import PartitionSpec as P

MESH = pl.DeviceIdType.MESH
INV_TEMP = 1.0 / 0.07
LOG2E = math.log2(math.e)
UP, DOWN, RIGHT, LEFT, TWIN = range(5)


def kernel(
    views, slots, desc_ref, match_ref, grad_ref, loss_ref, held, acc, loss, send_sem, recv_sem
):
    rows, width = desc_ref.shape
    chips = slots // 2
    extra = held.shape[2] - rows
    v = lax.axis_index("view")
    p = lax.axis_index("pix")
    x, c = p // 2, lax.rem(p, 2)
    there = {
        UP: (v + 1 < views, {"view": v + 1}),
        DOWN: (v >= 1, {"view": v - 1}),
        RIGHT: (x + 1 < chips, {"pix": p + 2}),
        LEFT: (x >= 1, {"pix": p - 2}),
        TWIN: (c >= 0, {"pix": p + 1 - 2 * c}),
    }

    barrier = pltpu.get_barrier_semaphore()
    count = 0
    for way in there:
        exists, target = there[way]

        @pl.when(exists)
        def _():
            pl.semaphore_signal(barrier, inc=1, device_id=target, device_id_type=MESH)

        count = count + exists.astype(jnp.int32)

    raw = desc_ref[...].astype(jnp.float32)
    scale = lax.rsqrt(jnp.mean(raw * raw, axis=-1, keepdims=True) + 1e-06) / math.sqrt(width)
    unit = raw * scale
    held[v, p, :rows, :] = unit.astype(jnp.bfloat16)
    own_links = match_ref[...]
    high = own_links // 256
    low = own_links - 256 * high
    links = jnp.concatenate([high, low], axis=0).astype(jnp.float32)
    links = jnp.concatenate([links, jnp.zeros((2 * views, width - rows), jnp.float32)], axis=1)
    if extra > 2 * views:
        links = jnp.concatenate([links, jnp.zeros((extra - 2 * views, width), jnp.float32)], axis=0)
    held[v, p, rows:, :] = links.astype(jnp.bfloat16)
    acc[...] = jnp.zeros_like(acc)
    loss[...] = jnp.zeros_like(loss)
    pl.semaphore_wait(barrier, count)

    def copy(way, view, slot):
        return pltpu.make_async_remote_copy(
            src_ref=held.at[view, slot],
            dst_ref=held.at[view, slot],
            send_sem=send_sem.at[way, view, slot],
            recv_sem=recv_sem.at[view, slot],
            device_id=there[way][1],
            device_id_type=MESH,
        )

    def send(way, view, slot):
        @pl.when(there[way][0])
        def _():
            copy(way, view, slot).start()

    def arrive(view, slot):
        copy(TWIN, view, slot).wait_recv()

    for way in (UP, DOWN, RIGHT, LEFT, TWIN):
        send(way, v, p)
    for step in range(1, chips):
        for sign, way in ((-1, RIGHT), (1, LEFT)):
            origin = x + sign * step

            @pl.when((origin >= 0) & (origin < chips))
            def _():
                slot = 2 * origin + c
                arrive(v, slot)
                for onward in (UP, DOWN, way, TWIN):
                    send(onward, v, slot)

    def forward(step):
        for q in range(chips):
            slot = 2 * q + c
            for sign, way in ((-1, UP), (1, DOWN)):
                view = v + sign * step

                @pl.when((view >= 0) & (view < views))
                def _():
                    arrive(view, slot)
                    send(way, view, slot)
                    send(TWIN, view, slot)

    def whole(view):
        return held[view, :, :rows, :].reshape(slots * rows, width)

    def exponent(left, right):
        dots = lax.dot_general(
            left, right, (((1,), (1,)), ((), ())), preferred_element_type=jnp.float32
        )
        return dots * (INV_TEMP * LOG2E)

    eye = lax.broadcasted_iota(jnp.int32, (rows, rows), 0) == lax.broadcasted_iota(
        jnp.int32, (rows, rows), 1
    )

    def compute(view):
        for q in range(chips):
            arrive(view, 2 * q + 1 - c)
        right = whole(view)
        power = exponent(held[v, p, :rows, :], right)
        expo = jnp.exp2(power)
        row_total = jnp.sum(expo, axis=1, keepdims=True)
        mine = match_ref[pl.ds(view, 1), :]
        mine = jnp.sum(jnp.where(eye, mine, 0).astype(jnp.float32), axis=1, keepdims=True)
        ids = lax.broadcasted_iota(jnp.int32, expo.shape, 1).astype(jnp.float32)
        row_hit = ids == mine
        positive = jnp.sum(jnp.where(row_hit, power, 0.0), axis=1, keepdims=True)
        loss[...] += jnp.log(row_total) - (1.0 / LOG2E) * positive

        def add(k, total):
            other = held[v, lax.rem(p + k, slots), :rows, :]
            return total + jnp.sum(
                jnp.exp2(exponent(other, right)), axis=0, keepdims=True
            )

        col_total = lax.fori_loop(1, slots, add, jnp.sum(expo, axis=0, keepdims=True))
        at = lax.broadcasted_iota(jnp.int32, (extra, width), 0)
        digit = jnp.where(at == v, 256.0, jnp.where(at == v + views, 1.0, 0.0))
        theirs = [
            jnp.sum(digit * held[view, s, rows:, :].astype(jnp.float32), axis=0, keepdims=True)[
                :, :rows
            ]
            for s in range(slots)
        ]
        theirs = jnp.concatenate(theirs, axis=1)
        own_ids = (lax.broadcasted_iota(jnp.int32, expo.shape, 0) + p * rows).astype(jnp.float32)
        col_hit = own_ids == theirs
        weight = expo * (1.0 / row_total + 1.0 / col_total)
        weight = weight - jnp.where(row_hit, 1.0, 0.0) - jnp.where(col_hit, 1.0, 0.0)
        acc[...] += jnp.dot(
            weight.astype(jnp.bfloat16), right, preferred_element_type=jnp.float32
        )

    def both(step):
        def one(k, carry):
            view = v + step * (2 * k - 1)

            @pl.when((view >= 0) & (view < views))
            def _():
                compute(view)

            return carry

        lax.fori_loop(0, 2, one, 0)

    def round_of(step, carry):
        @pl.when(step < views)
        def _():
            forward(step)

        @pl.when(step == 1)
        def _():
            for q in range(chips):
                arrive(v, 2 * q + 1 - c)

        @pl.when(step >= 2)
        def _():
            both(step - 1)

        return carry

    lax.fori_loop(1, views + 1, round_of, 0)

    unit_grad = (INV_TEMP / (views - 1)) * acc[...]
    raw = desc_ref[...].astype(jnp.float32)
    scale = lax.rsqrt(jnp.mean(raw * raw, axis=-1, keepdims=True) + 1e-06) / math.sqrt(width)
    unit = raw * scale
    along = jnp.sum(unit * unit_grad, axis=-1, keepdims=True)
    grad_ref[...] = (scale * (unit_grad - unit * along)).astype(jnp.bfloat16)
    loss_ref[...] = jnp.sum(
        jnp.where(eye, loss[...] * (1.0 / (views - 1)), 0.0), axis=0, keepdims=True
    )

    def sent(way, view, slot):
        @pl.when(there[way][0])
        def _():
            copy(way, view, slot).wait_send()

    def drain(view, carry):
        for q in range(chips):
            slot = 2 * q + c
            sent(TWIN, view, slot)

            @pl.when(view <= v)
            def _():
                sent(UP, view, slot)

            @pl.when(view >= v)
            def _():
                sent(DOWN, view, slot)

        return carry

    lax.fori_loop(0, views, drain, 0)
    for q in range(chips):

        @pl.when(q <= x)
        def _():
            sent(RIGHT, v, 2 * q + c)

        @pl.when(q >= x)
        def _():
            sent(LEFT, v, 2 * q + c)


def body(views, slots, descriptors, matches):
    rows, width = descriptors.shape[1:]
    extra = -(-2 * views // 16) * 16
    grad, loss = pl.pallas_call(
        functools.partial(kernel, views, slots),
        out_shape=(
            jax.ShapeDtypeStruct((rows, width), jnp.bfloat16),
            jax.ShapeDtypeStruct((1, rows), jnp.float32),
        ),
        in_specs=[pl.BlockSpec(memory_space=pltpu.VMEM)] * 2,
        out_specs=(pl.BlockSpec(memory_space=pltpu.VMEM),) * 2,
        scratch_shapes=[
            pltpu.VMEM((views, slots, rows + extra, width), jnp.bfloat16),
            pltpu.VMEM((rows, width), jnp.float32),
            pltpu.VMEM((rows, 1), jnp.float32),
            pltpu.SemaphoreType.DMA((5, views, slots)),
            pltpu.SemaphoreType.DMA((views, slots)),
        ],
        compiler_params=pltpu.CompilerParams(
            collective_id=0, has_side_effects=True, vmem_limit_bytes=48 * 1024 * 1024
        ),
        cost_estimate=pl.CostEstimate(
            flops=2 * (slots + 1) * rows * (views - 1) * slots * rows * width,
            bytes_accessed=4 * rows * width,
            transcendentals=slots * rows * (views - 1) * slots * rows,
        ),
    )(descriptors[0], matches[0])
    return grad[None], loss


def solution(mesh):
    views, slots = mesh.shape["view"], mesh.shape["pix"]
    in_specs = (P(("parts", "view"), "pix", None), P(("parts", "view"), None, "pix"))
    out_specs = (P(("parts", "view"), "pix", None), P(("parts", "view"), "pix"))
    return jax.shard_map(
        functools.partial(body, views, slots),
        mesh=mesh, in_specs=in_specs, out_specs=out_specs, check_vma=False,
    )
```

time: 154 us -> 28.4 us (0.18)
  the two profiles are of different devices: /device:TPU:1 before, /device:TPU:0 now
where the time goes in v1:
time: 28.4 us; the launch traced here: 28.2 us
  Pallas kernels  24.8 us (87%)
  local copies, waits for them, and re-layouts  2.78 us (10%)
  between operations  0.65 us (2%)
    pallas_call x1, Pallas kernels, body(): pl.pallas_call(functools.partial(kernel, views, slots), out_shape=(jax.Sh...  24.8 us
    unnamed x6, local copies, waits for them, and re-layouts  2.78 us

profile of v1, /device:TPU:0, one launch (start us, length us, event | category | flops | bytes accessed | tf_op | source)
XLA Modules:
  0.0 28.2 jit_solution(2817613251748860757)
XLA Ops:
  0.6 0.0 copy-start
  0.6 0.9 %copy-done = bf16[1,192,256]{2,1,0:T(8,128)(2,1)S(1)} copy-done((bf16[1,192,256]{2,1,0:T(8,128)(2,1)S(1)}, bf16[1,192,256]{2,1,0:T(8,128)(2,1)}, u32[]{:S(2)}) %copy-start) | copy-done | bytes 98328
  1.5 0.0 copy-start.1
  1.5 0.7 %copy-done.1 = s32[1,4,192]{2,1,0:T(4,128)S(1)} copy-done((s32[1,4,192]{2,1,0:T(4,128)S(1)}, s32[1,4,192]{2,1,0:T(4,128)}, u32[]{:S(2)}) %copy-start.1) | copy-done | bytes 3096
  2.2 24.8 %shard_map.41 = (bf16[192,256]{1,0:T(8,128)(2,1)S(1)}, f32[1,192]{1,0:T(1,128)S(1)}) custom-call(bf16[192,256]{1,0:T(8,128)(2,1)S(1)} %bitcast.4, s32[4,192]{1,0:T(4,128)S(1)} %bitcast.5), custom_call_target="tpu_custom_call" | custom-call | flops 1132462080 | bytes 196608 | tf_op jit(solution)/shard_map/pallas_call | solution.py:230
  27.0 0.6 %copy.6 = bf16[1,192,256]{2,1,0:T(8,128)(2,1)} copy(bf16[1,192,256]{2,1,0:T(8,128)(2,1)S(1)} %bitcast.3) | data formatting | bytes 196608
  27.7 0.6 %copy.7 = f32[1,192]{1,0:T(1,128)} copy(f32[1,192]{1,0:T(1,128)S(1)} %get-tuple-element.9) | data formatting | bytes 1536
Async XLA Ops:
  0.6 0.9 %copy-start = (bf16[1,192,256]{2,1,0:T(8,128)(2,1)S(1)}, bf16[1,192,256]{2,1,0:T(8,128)(2,1)}, u32[]{:S(2)}) copy-start(bf16[1,192,256]{2,1,0:T(8,128)(2,1)} %param.2) | copy-start | bytes 294916
  1.5 0.7 %copy-start.1 = (s32[1,4,192]{2,1,0:T(4,128)S(1)}, s32[1,4,192]{2,1,0:T(4,128)}, u32[]{:S(2)}) copy-start(s32[1,4,192]{2,1,0:T(4,128)} %param.3) | copy-start | bytes 9220

commit v2 on v1

v2 whole, which is shorter than its diff:
```python
import functools
import math

import jax
import jax.numpy as jnp
from jax import lax
from jax.experimental import pallas as pl
from jax.experimental.pallas import tpu as pltpu
from jax.sharding import PartitionSpec as P

MESH = pl.DeviceIdType.MESH
INV_TEMP = 1.0 / 0.07
LOG2E = math.log2(math.e)
CHUNKS = 1
UP, DOWN, RIGHT, LEFT, TWIN = range(5)


def kernel(
    views, slots, desc_any, match_any, grad_ref, loss_ref,
    desc_ref, match_ref, held, acc, loss, expos, rest, row_total, load_sem, send_sem, recv_sem,
):
    loads = [
        pltpu.make_async_copy(desc_any, desc_ref, load_sem.at[0]),
        pltpu.make_async_copy(match_any, match_ref, load_sem.at[1]),
    ]
    for load in loads:
        load.start()
    rows, width = desc_ref.shape
    chips = slots // 2
    extra = held.shape[2] - rows
    tiles = (rows + extra) // 16
    cuts = [16 * (tiles * k // CHUNKS) for k in range(CHUNKS + 1)]
    v = lax.axis_index("view")
    p = lax.axis_index("pix")
    x, c = p // 2, lax.rem(p, 2)
    there = {
        UP: (v + 1 < views, {"view": v + 1}),
        DOWN: (v >= 1, {"view": v - 1}),
        RIGHT: (x + 1 < chips, {"pix": p + 2}),
        LEFT: (x >= 1, {"pix": p - 2}),
        TWIN: (c >= 0, {"pix": p + 1 - 2 * c}),
    }

    barrier = pltpu.get_barrier_semaphore()
    count = 0
    for way in there:
        exists, target = there[way]

        @pl.when(exists)
        def _():
            pl.semaphore_signal(barrier, inc=1, device_id=target, device_id_type=MESH)

        count = count + exists.astype(jnp.int32)

    for load in loads:
        load.wait()
    raw = desc_ref[...].astype(jnp.float32)
    scale = lax.rsqrt(jnp.mean(raw * raw, axis=-1, keepdims=True) + 1e-06) / math.sqrt(width)
    unit = raw * scale
    held[v, p, :rows, :] = unit.astype(jnp.bfloat16)
    own_links = match_ref[...]
    high = own_links // 256
    low = own_links - 256 * high
    links = jnp.concatenate([high, low], axis=0).astype(jnp.float32)
    links = jnp.concatenate([links, jnp.zeros((2 * views, width - rows), jnp.float32)], axis=1)
    if extra > 2 * views:
        links = jnp.concatenate([links, jnp.zeros((extra - 2 * views, width), jnp.float32)], axis=0)
    held[v, p, rows:, :] = links.astype(jnp.bfloat16)
    acc[...] = jnp.zeros_like(acc)
    loss[...] = jnp.zeros_like(loss)
    pl.semaphore_wait(barrier, count)

    def piece(view, slot, k):
        return held.at[view, slot, pl.ds(cuts[k], cuts[k + 1] - cuts[k])]

    def copy(way, view, slot, k):
        return pltpu.make_async_remote_copy(
            src_ref=piece(view, slot, k),
            dst_ref=piece(view, slot, k),
            send_sem=send_sem.at[way, view, slot, k],
            recv_sem=recv_sem.at[view, slot, k],
            device_id=there[way][1],
            device_id_type=MESH,
        )

    def send(way, view, slot, k):
        @pl.when(there[way][0])
        def _():
            copy(way, view, slot, k).start()

    def arrive(view, slot, k):
        copy(TWIN, view, slot, k).wait_recv()

    def sides(step, act):
        for sign, onward in ((-1, UP), (1, DOWN)):
            view = v + sign * step

            @pl.when((view >= 0) & (view < views))
            def _():
                act(view, onward)

    for k in range(CHUNKS):
        for way in (UP, DOWN, RIGHT, LEFT, TWIN):
            send(way, v, p, k)

    def along_view(step):
        def act(view, onward):
            for k in range(CHUNKS):
                arrive(view, p, k)
                for way in (onward, RIGHT, LEFT, TWIN):
                    send(way, view, p, k)

        sides(step, act)

    def along_x(view):
        for step in range(1, chips):
            for sign, way in ((-1, RIGHT), (1, LEFT)):
                origin = x + sign * step

                @pl.when((origin >= 0) & (origin < chips))
                def _():
                    slot = 2 * origin + c
                    for k in range(CHUNKS):
                        arrive(view, slot, k)
                        send(way, view, slot, k)
                        send(TWIN, view, slot, k)

    def from_twin(view, q):
        for k in range(CHUNKS):
            arrive(view, 2 * q + 1 - c, k)

    def pair(view, q):
        return held[view, pl.ds(2 * q, 2), :rows, :].reshape(2 * rows, width)

    def exponent(left, right):
        dots = lax.dot_general(
            left, right, (((1,), (1,)), ((), ())), preferred_element_type=jnp.float32
        )
        return dots * (INV_TEMP * LOG2E)

    eye = lax.broadcasted_iota(jnp.int32, (rows, rows), 0) == lax.broadcasted_iota(
        jnp.int32, (rows, rows), 1
    )

    def half(view, place, q):
        from_twin(view, q)
        right = pair(view, q)
        power = exponent(held[v, p, :rows, :], right)
        expo = jnp.exp2(power)
        row_total[place] += jnp.sum(expo, axis=1, keepdims=True)
        mine = match_ref[pl.ds(view, 1), :]
        mine = jnp.sum(jnp.where(eye, mine, 0).astype(jnp.float32), axis=1, keepdims=True)
        first = (2 * q * rows).astype(jnp.float32)
        ids = lax.broadcasted_iota(jnp.int32, expo.shape, 1).astype(jnp.float32) + first
        row_hit = ids == mine
        loss[...] -= (1.0 / LOG2E) * jnp.sum(
            jnp.where(row_hit, power, 0.0), axis=1, keepdims=True
        )

        def add(k, total):
            other = held[v, lax.rem(p + k, slots), :rows, :]
            return total + jnp.sum(jnp.exp2(exponent(other, right)), axis=0, keepdims=True)

        col_total = lax.fori_loop(
            1, slots, add, jnp.sum(expo, axis=0, keepdims=True), unroll=slots <= 4
        )
        at = lax.broadcasted_iota(jnp.int32, (extra, width), 0)
        digit = jnp.where(at == v, 256.0, jnp.where(at == v + views, 1.0, 0.0))
        theirs = [
            jnp.sum(
                digit * held[view, 2 * q + s, rows:, :].astype(jnp.float32), axis=0, keepdims=True
            )[:, :rows]
            for s in range(2)
        ]
        theirs = jnp.concatenate(theirs, axis=1)
        own_ids = (lax.broadcasted_iota(jnp.int32, expo.shape, 0) + p * rows).astype(jnp.float32)
        col_hit = own_ids == theirs
        expos[place, q] = expo
        rest[place, q] = (
            expo * (1.0 / col_total) - jnp.where(row_hit, 1.0, 0.0) - jnp.where(col_hit, 1.0, 0.0)
        )

    def finish(view, place):
        total = row_total[place]
        row_total[place] = jnp.zeros_like(total)
        loss[...] += jnp.log(total)
        inverse = 1.0 / total

        def one(q, carry):
            weight = expos[place, q] * inverse + rest[place, q]
            acc[...] += jnp.dot(
                weight.astype(jnp.bfloat16), pair(view, q), preferred_element_type=jnp.float32
            )
            return carry

        lax.fori_loop(0, chips, one, 0, unroll=chips <= 2)

    row_total[...] = jnp.zeros_like(row_total)

    def round_of(step, carry):
        @pl.when(step < views)
        def _():
            along_view(step)

        @pl.when(step == 1)
        def _():
            along_x(v)
            for q in range(chips):
                from_twin(v, q)

        @pl.when(step > 1)
        def _():
            sides(step - 1, lambda view, onward: along_x(view))

        def work(k, carry):
            late = (k // 2) == 0
            away = jnp.where(late, step - 1, step)
            side = lax.rem(k, 2)
            view = v + away * (2 * side - 1)
            place = 2 * lax.rem(away, 2) + side
            fine = (view >= 0) & (view < views) & (away >= 1) & (away < views)

            def part(n, carry):
                half(view, place, lax.rem(x + n, chips))
                return carry

            @pl.when(fine)
            def _():
                lax.fori_loop(jnp.where(late, 1, 0), jnp.where(late, chips, 1), part, 0)

            @pl.when(fine & late)
            def _():
                finish(view, place)

            return carry

        lax.fori_loop(0, 4, work, 0)
        return carry

    lax.fori_loop(1, views + 1, round_of, 0)

    unit_grad = (INV_TEMP / (views - 1)) * acc[...]
    raw = desc_ref[...].astype(jnp.float32)
    scale = lax.rsqrt(jnp.mean(raw * raw, axis=-1, keepdims=True) + 1e-06) / math.sqrt(width)
    unit = raw * scale
    along = jnp.sum(unit * unit_grad, axis=-1, keepdims=True)
    grad_ref[...] = (scale * (unit_grad - unit * along)).astype(jnp.bfloat16)
    loss_ref[...] = jnp.sum(
        jnp.where(eye, loss[...] * (1.0 / (views - 1)), 0.0), axis=0, keepdims=True
    )

    def sent(way, view, slot):
        @pl.when(there[way][0])
        def _():
            for k in range(CHUNKS):
                copy(way, view, slot, k).wait_send()

    def drain(view, carry):
        @pl.when(view <= v)
        def _():
            sent(UP, view, p)

        @pl.when(view >= v)
        def _():
            sent(DOWN, view, p)

        for q in range(chips):
            slot = 2 * q + c
            sent(TWIN, view, slot)

            @pl.when(q <= x)
            def _():
                sent(RIGHT, view, slot)

            @pl.when(q >= x)
            def _():
                sent(LEFT, view, slot)

        return carry

    lax.fori_loop(0, views, drain, 0)


def body(views, slots, descriptors, matches):
    rows, width = descriptors.shape[1:]
    extra = -(-2 * views // 16) * 16
    grad, loss = pl.pallas_call(
        functools.partial(kernel, views, slots),
        out_shape=(
            jax.ShapeDtypeStruct((rows, width), jnp.bfloat16),
            jax.ShapeDtypeStruct((1, rows), jnp.float32),
        ),
        in_specs=[pl.BlockSpec(memory_space=pl.ANY)] * 2,
        out_specs=(pl.BlockSpec(memory_space=pltpu.VMEM),) * 2,
        scratch_shapes=[
            pltpu.VMEM((rows, width), jnp.bfloat16),
            pltpu.VMEM((views, rows), jnp.int32),
            pltpu.VMEM((views, slots, rows + extra, width), jnp.bfloat16),
            pltpu.VMEM((rows, width), jnp.float32),
            pltpu.VMEM((rows, 1), jnp.float32),
            pltpu.VMEM((4, slots // 2, rows, 2 * rows), jnp.float32),
            pltpu.VMEM((4, slots // 2, rows, 2 * rows), jnp.float32),
            pltpu.VMEM((4, rows, 1), jnp.float32),
            pltpu.SemaphoreType.DMA((2,)),
            pltpu.SemaphoreType.DMA((5, views, slots, CHUNKS)),
            pltpu.SemaphoreType.DMA((views, slots, CHUNKS)),
        ],
        compiler_params=pltpu.CompilerParams(
            collective_id=0, has_side_effects=True, vmem_limit_bytes=48 * 1024 * 1024
        ),
        cost_estimate=pl.CostEstimate(
            flops=2 * (slots + 1) * rows * (views - 1) * slots * rows * width,
            bytes_accessed=4 * rows * width,
            transcendentals=slots * rows * (views - 1) * slots * rows,
        ),
    )(descriptors[0], matches[0])
    return grad[None], loss


def solution(mesh):
    views, slots = mesh.shape["view"], mesh.shape["pix"]
    in_specs = (P(("parts", "view"), "pix", None), P(("parts", "view"), None, "pix"))
    out_specs = (P(("parts", "view"), "pix", None), P(("parts", "view"), "pix"))
    return jax.shard_map(
        functools.partial(body, views, slots),
        mesh=mesh, in_specs=in_specs, out_specs=out_specs, check_vma=False,
    )
```

time: 28.4 us -> 26.1 us (0.919)
  the two profiles are of different devices: /device:TPU:0 before, /device:TPU:1 now
where the time goes in v2:
time: 26.1 us; the launch traced here: 25.9 us
  Pallas kernels  22.5 us (86%)
  local copies, waits for them, and re-layouts  2.78 us (11%)
  between operations  0.65 us (2%)
    pallas_call x1, Pallas kernels, body(): pl.pallas_call(functools.partial(kernel, views, slots), out_shape=(jax.Sh...  22.5 us
    unnamed x6, local copies, waits for them, and re-layouts  2.78 us

profile of v2, /device:TPU:1, one launch (start us, length us, event | category | flops | bytes accessed | tf_op | source)
XLA Modules:
  0.0 25.9 jit_solution(7528191846501841382)
XLA Ops:
  0.6 0.0 copy-start
  0.6 0.9 %copy-done = bf16[1,192,256]{2,1,0:T(8,128)(2,1)S(1)} copy-done((bf16[1,192,256]{2,1,0:T(8,128)(2,1)S(1)}, bf16[1,192,256]{2,1,0:T(8,128)(2,1)}, u32[]{:S(2)}) %copy-start) | copy-done | bytes 98328
  1.5 0.0 copy-start.1
  1.5 0.7 %copy-done.1 = s32[1,4,192]{2,1,0:T(4,128)S(1)} copy-done((s32[1,4,192]{2,1,0:T(4,128)S(1)}, s32[1,4,192]{2,1,0:T(4,128)}, u32[]{:S(2)}) %copy-start.1) | copy-done | bytes 3096
  2.2 22.5 %shard_map.41 = (bf16[192,256]{1,0:T(8,128)(2,1)S(1)}, f32[1,192]{1,0:T(1,128)S(1)}) custom-call(bf16[192,256]{1,0:T(8,128)(2,1)S(1)} %bitcast.4, s32[4,192]{1,0:T(4,128)S(1)} %bitcast.5), custom_call_target="tpu_custom_call" | custom-call | flops 1132462080 | bytes 196608 | tf_op jit(solution)/shard_map/pallas_call | solution.py:287
  24.7 0.6 %copy.6 = bf16[1,192,256]{2,1,0:T(8,128)(2,1)} copy(bf16[1,192,256]{2,1,0:T(8,128)(2,1)S(1)} %bitcast.3) | data formatting | bytes 196608
  25.3 0.6 %copy.7 = f32[1,192]{1,0:T(1,128)} copy(f32[1,192]{1,0:T(1,128)S(1)} %get-tuple-element.9) | data formatting | bytes 1536
Async XLA Ops:
  0.6 0.9 %copy-start = (bf16[1,192,256]{2,1,0:T(8,128)(2,1)S(1)}, bf16[1,192,256]{2,1,0:T(8,128)(2,1)}, u32[]{:S(2)}) copy-start(bf16[1,192,256]{2,1,0:T(8,128)(2,1)} %param.2) | copy-start | bytes 294916
  1.5 0.7 %copy-start.1 = (s32[1,4,192]{2,1,0:T(4,128)S(1)}, s32[1,4,192]{2,1,0:T(4,128)}, u32[]{:S(2)}) copy-start(s32[1,4,192]{2,1,0:T(4,128)} %param.3) | copy-start | bytes 9220

commit v3 on v2

--- a/solution.py
+++ b/solution.py
@@ -16,15 +16,9 @@
 
 
 def kernel(
-    views, slots, desc_any, match_any, grad_ref, loss_ref,
-    desc_ref, match_ref, held, acc, loss, expos, rest, row_total, load_sem, send_sem, recv_sem,
+    views, slots, desc_ref, match_ref, grad_ref, loss_ref,
+    held, acc, loss, expos, rest, row_total, send_sem, recv_sem,
 ):
-    loads = [
-        pltpu.make_async_copy(desc_any, desc_ref, load_sem.at[0]),
-        pltpu.make_async_copy(match_any, match_ref, load_sem.at[1]),
-    ]
-    for load in loads:
-        load.start()
     rows, width = desc_ref.shape
     chips = slots // 2
     extra = held.shape[2] - rows
@@ -52,8 +46,6 @@
 
         count = count + exists.astype(jnp.int32)
 
-    for load in loads:
-        load.wait()
     raw = desc_ref[...].astype(jnp.float32)
     scale = lax.rsqrt(jnp.mean(raw * raw, axis=-1, keepdims=True) + 1e-06) / math.sqrt(width)
     unit = raw * scale
@@ -290,18 +282,15 @@
             jax.ShapeDtypeStruct((rows, width), jnp.bfloat16),
             jax.ShapeDtypeStruct((1, rows), jnp.float32),
         ),
-        in_specs=[pl.BlockSpec(memory_space=pl.ANY)] * 2,
+        in_specs=[pl.BlockSpec(memory_space=pltpu.VMEM)] * 2,
         out_specs=(pl.BlockSpec(memory_space=pltpu.VMEM),) * 2,
         scratch_shapes=[
-            pltpu.VMEM((rows, width), jnp.bfloat16),
-            pltpu.VMEM((views, rows), jnp.int32),
             pltpu.VMEM((views, slots, rows + extra, width), jnp.bfloat16),
             pltpu.VMEM((rows, width), jnp.float32),
             pltpu.VMEM((rows, 1), jnp.float32),
             pltpu.VMEM((4, slots // 2, rows, 2 * rows), jnp.float32),
             pltpu.VMEM((4, slots // 2, rows, 2 * rows), jnp.float32),
             pltpu.VMEM((4, rows, 1), jnp.float32),
-            pltpu.SemaphoreType.DMA((2,)),
             pltpu.SemaphoreType.DMA((5, views, slots, CHUNKS)),
             pltpu.SemaphoreType.DMA((views, slots, CHUNKS)),
         ],

time: 26.1 us -> 25.9 us (level)
  no operation moved by 1% of the time
where the time goes in v3:
time: 25.9 us; the launch traced here: 25.7 us
  Pallas kernels  22.3 us (86%)
  local copies, waits for them, and re-layouts  2.78 us (11%)
  between operations  0.65 us (3%)
    pallas_call x1, Pallas kernels, body(): pl.pallas_call(functools.partial(kernel, views, slots), out_shape=(jax.Sh...  22.3 us
    unnamed x6, local copies, waits for them, and re-layouts  2.78 us

profile of v3, /device:TPU:1, one launch (start us, length us, event | category | flops | bytes accessed | tf_op | source)
XLA Modules:
  0.0 25.7 jit_solution(9838653127679722972)
XLA Ops:
  0.6 0.0 copy-start
  0.6 0.9 %copy-done = bf16[1,192,256]{2,1,0:T(8,128)(2,1)S(1)} copy-done((bf16[1,192,256]{2,1,0:T(8,128)(2,1)S(1)}, bf16[1,192,256]{2,1,0:T(8,128)(2,1)}, u32[]{:S(2)}) %copy-start) | copy-done | bytes 98328
  1.5 0.0 copy-start.1
  1.5 0.7 %copy-done.1 = s32[1,4,192]{2,1,0:T(4,128)S(1)} copy-done((s32[1,4,192]{2,1,0:T(4,128)S(1)}, s32[1,4,192]{2,1,0:T(4,128)}, u32[]{:S(2)}) %copy-start.1) | copy-done | bytes 3096
  2.2 22.3 %shard_map.41 = (bf16[192,256]{1,0:T(8,128)(2,1)S(1)}, f32[1,192]{1,0:T(1,128)S(1)}) custom-call(bf16[192,256]{1,0:T(8,128)(2,1)S(1)} %bitcast.4, s32[4,192]{1,0:T(4,128)S(1)} %bitcast.5), custom_call_target="tpu_custom_call" | custom-call | flops 1132462080 | bytes 196608 | tf_op jit(solution)/shard_map/pallas_call | solution.py:279
  24.5 0.6 %copy.6 = bf16[1,192,256]{2,1,0:T(8,128)(2,1)} copy(bf16[1,192,256]{2,1,0:T(8,128)(2,1)S(1)} %bitcast.3) | data formatting | bytes 196608
  25.2 0.6 %copy.7 = f32[1,192]{1,0:T(1,128)} copy(f32[1,192]{1,0:T(1,128)S(1)} %get-tuple-element.9) | data formatting | bytes 1536
Async XLA Ops:
  0.6 0.9 %copy-start = (bf16[1,192,256]{2,1,0:T(8,128)(2,1)S(1)}, bf16[1,192,256]{2,1,0:T(8,128)(2,1)}, u32[]{:S(2)}) copy-start(bf16[1,192,256]{2,1,0:T(8,128)(2,1)} %param.2) | copy-start | bytes 294916
  1.5 0.7 %copy-start.1 = (s32[1,4,192]{2,1,0:T(4,128)S(1)}, s32[1,4,192]{2,1,0:T(4,128)}, u32[]{:S(2)}) copy-start(s32[1,4,192]{2,1,0:T(4,128)} %param.3) | copy-start | bytes 9220

commit v4 on v2

--- a/solution.py
+++ b/solution.py
@@ -290,7 +290,7 @@
             jax.ShapeDtypeStruct((rows, width), jnp.bfloat16),
             jax.ShapeDtypeStruct((1, rows), jnp.float32),
         ),
-        in_specs=[pl.BlockSpec(memory_space=pl.ANY)] * 2,
+        in_specs=[pl.BlockSpec(memory_space=pltpu.HBM)] * 2,
         out_specs=(pl.BlockSpec(memory_space=pltpu.VMEM),) * 2,
         scratch_shapes=[
             pltpu.VMEM((rows, width), jnp.bfloat16),

time: 26.1 us -> 26.1 us (level)
  no operation moved by 1% of the time
where the time goes in v4:
time: 26.1 us; the launch traced here: 25.9 us
  Pallas kernels  22.5 us (86%)
  local copies, waits for them, and re-layouts  2.78 us (11%)
  between operations  0.65 us (2%)
    pallas_call x1, Pallas kernels, body(): pl.pallas_call(functools.partial(kernel, views, slots), out_shape=(jax.Sh...  22.5 us
    unnamed x6, local copies, waits for them, and re-layouts  2.78 us

profile of v4, /device:TPU:1, one launch (start us, length us, event | category | flops | bytes accessed | tf_op | source)
XLA Modules:
  0.0 25.9 jit_solution(7528191846501841382)
XLA Ops:
  0.6 0.0 copy-start
  0.6 0.9 %copy-done = bf16[1,192,256]{2,1,0:T(8,128)(2,1)S(1)} copy-done((bf16[1,192,256]{2,1,0:T(8,128)(2,1)S(1)}, bf16[1,192,256]{2,1,0:T(8,128)(2,1)}, u32[]{:S(2)}) %copy-start) | copy-done | bytes 98328
  1.5 0.0 copy-start.1
  1.5 0.7 %copy-done.1 = s32[1,4,192]{2,1,0:T(4,128)S(1)} copy-done((s32[1,4,192]{2,1,0:T(4,128)S(1)}, s32[1,4,192]{2,1,0:T(4,128)}, u32[]{:S(2)}) %copy-start.1) | copy-done | bytes 3096
  2.2 22.5 %shard_map.41 = (bf16[192,256]{1,0:T(8,128)(2,1)S(1)}, f32[1,192]{1,0:T(1,128)S(1)}) custom-call(bf16[192,256]{1,0:T(8,128)(2,1)S(1)} %bitcast.4, s32[4,192]{1,0:T(4,128)S(1)} %bitcast.5), custom_call_target="tpu_custom_call" | custom-call | flops 1132462080 | bytes 196608 | tf_op jit(solution)/shard_map/pallas_call | solution.py:287
  24.7 0.6 %copy.6 = bf16[1,192,256]{2,1,0:T(8,128)(2,1)} copy(bf16[1,192,256]{2,1,0:T(8,128)(2,1)S(1)} %bitcast.3) | data formatting | bytes 196608
  25.3 0.6 %copy.7 = f32[1,192]{1,0:T(1,128)} copy(f32[1,192]{1,0:T(1,128)S(1)} %get-tuple-element.9) | data formatting | bytes 1536
Async XLA Ops:
  0.6 0.9 %copy-start = (bf16[1,192,256]{2,1,0:T(8,128)(2,1)S(1)}, bf16[1,192,256]{2,1,0:T(8,128)(2,1)}, u32[]{:S(2)}) copy-start(bf16[1,192,256]{2,1,0:T(8,128)(2,1)} %param.2) | copy-start | bytes 294916
  1.5 0.7 %copy-start.1 = (s32[1,4,192]{2,1,0:T(4,128)S(1)}, s32[1,4,192]{2,1,0:T(4,128)}, u32[]{:S(2)}) copy-start(s32[1,4,192]{2,1,0:T(4,128)} %param.3) | copy-start | bytes 9220

commit v5 on v3

--- a/solution.py
+++ b/solution.py
@@ -11,7 +11,7 @@
 MESH = pl.DeviceIdType.MESH
 INV_TEMP = 1.0 / 0.07
 LOG2E = math.log2(math.e)
-CHUNKS = 1
+CHUNKS = 2
 UP, DOWN, RIGHT, LEFT, TWIN = range(5)
 
 
@@ -99,7 +99,7 @@
         def act(view, onward):
             for k in range(CHUNKS):
                 arrive(view, p, k)
-                for way in (onward, RIGHT, LEFT, TWIN):
+                for way in (onward, TWIN, RIGHT, LEFT):
                     send(way, view, p, k)
 
         sides(step, act)

time: 25.9 us -> 25.9 us (level)
  no operation moved by 1% of the time
where the time goes in v5:
time: 25.9 us; the launch traced here: 25.7 us
  Pallas kernels  22.3 us (86%)
  local copies, waits for them, and re-layouts  2.78 us (11%)
  between operations  0.65 us (3%)
    pallas_call x1, Pallas kernels, body(): pl.pallas_call(functools.partial(kernel, views, slots), out_shape=(jax.Sh...  22.3 us
    unnamed x6, local copies, waits for them, and re-layouts  2.78 us

profile of v5, /device:TPU:1, one launch (start us, length us, event | category | flops | bytes accessed | tf_op | source)
XLA Modules:
  0.0 25.7 jit_solution(1634937938756463837)
XLA Ops:
  0.6 0.0 copy-start
  0.6 0.9 %copy-done = bf16[1,192,256]{2,1,0:T(8,128)(2,1)S(1)} copy-done((bf16[1,192,256]{2,1,0:T(8,128)(2,1)S(1)}, bf16[1,192,256]{2,1,0:T(8,128)(2,1)}, u32[]{:S(2)}) %copy-start) | copy-done | bytes 98328
  1.5 0.0 copy-start.1
  1.5 0.7 %copy-done.1 = s32[1,4,192]{2,1,0:T(4,128)S(1)} copy-done((s32[1,4,192]{2,1,0:T(4,128)S(1)}, s32[1,4,192]{2,1,0:T(4,128)}, u32[]{:S(2)}) %copy-start.1) | copy-done | bytes 3096
  2.2 22.3 %shard_map.41 = (bf16[192,256]{1,0:T(8,128)(2,1)S(1)}, f32[1,192]{1,0:T(1,128)S(1)}) custom-call(bf16[192,256]{1,0:T(8,128)(2,1)S(1)} %bitcast.4, s32[4,192]{1,0:T(4,128)S(1)} %bitcast.5), custom_call_target="tpu_custom_call" | custom-call | flops 1132462080 | bytes 196608 | tf_op jit(solution)/shard_map/pallas_call | solution.py:279
  24.5 0.6 %copy.6 = bf16[1,192,256]{2,1,0:T(8,128)(2,1)} copy(bf16[1,192,256]{2,1,0:T(8,128)(2,1)S(1)} %bitcast.3) | data formatting | bytes 196608
  25.1 0.6 %copy.7 = f32[1,192]{1,0:T(1,128)} copy(f32[1,192]{1,0:T(1,128)S(1)} %get-tuple-element.9) | data formatting | bytes 1536
Async XLA Ops:
  0.6 0.9 %copy-start = (bf16[1,192,256]{2,1,0:T(8,128)(2,1)S(1)}, bf16[1,192,256]{2,1,0:T(8,128)(2,1)}, u32[]{:S(2)}) copy-start(bf16[1,192,256]{2,1,0:T(8,128)(2,1)} %param.2) | copy-start | bytes 294916
  1.5 0.7 %copy-start.1 = (s32[1,4,192]{2,1,0:T(4,128)S(1)}, s32[1,4,192]{2,1,0:T(4,128)}, u32[]{:S(2)}) copy-start(s32[1,4,192]{2,1,0:T(4,128)} %param.3) | copy-start | bytes 9220
